TPU v7x, 256 devices: a whole 4x4x8 slice. The times are simulated.
256 devices in a mesh: dp: 16 (over y_lo, x, core), ref: 16 (over z, y_hi).
Axes of the slice: x: 4, y: 4 (y_hi: 2, y_lo: 2; y = y_hi * 2 + y_lo), z: 8, core: 2. Of those that a mesh axis runs over, the one named last changes fastest.
Arguments:
- images: bfloat16 [12288, 16384], P(('dp', 'ref'))
- ctf: bfloat16 [12288, 8192], P(('dp', 'ref'))
- refs: bfloat16 [192, 16384], P('ref')
- shifts: int32 [9, 2], replicated, may hold values from -3 to 3
- lists: int32 [12288, 12], P(('dp', 'ref')), may hold values from 0 to 191, as said below
- counts: int32 [12288], P(('dp', 'ref')), may hold values from 1 to 12
Outputs:
- sums: float32 [192, 16384], P('ref', 'dp')
- totals: float32 [192], P('ref')
- log_evidence: float32 [12288], P(('dp', 'ref'))
Inputs may be any that keep to these rules, and one draw needn't show every extreme that they name: Row p of lists holds 12 distinct orientation indices, clustered near one orientation; only its first counts[p] entries are used.
All inputs are finite; a program needn't handle non-finite values.
Results may differ from a plain program's by a relative error of at most 0.0045.
Values may be sent and summed in bfloat16 or wider, within the bound.
No kernel may reach another device: no remote copies, remote signals or barrier semaphores. Data moves between devices by JAX's collectives and lax.ppermute only.
A program may use at most 128 MiB of HBM per device.

v0:
```python
import math

import jax
import jax.numpy as jnp
from jax import lax
from jax.sharding import PartitionSpec as P

GRID = 128


def from_behind(value, axis, steps):
    count = lax.axis_size(axis)
    pairs = [(source, (source + steps) % count) for source in range(count)]
    return lax.ppermute(value, axis, pairs)


def phase_tables(shifts, pixels):
    half = GRID // 2
    pixel = jnp.arange(pixels, dtype=jnp.int32)
    row = pixel // half
    column = pixel % half
    freq_y = (row + half) % GRID - half
    turns = (column[None, :] * shifts[:, 0:1] + freq_y[None, :] * shifts[:, 1:2]) % GRID
    angle = turns.astype(jnp.float32) * jnp.float32(2.0 * math.pi / GRID)
    return (jnp.cos(angle), jnp.sin(angle))


def local(images, ctf, refs, shifts, lists, counts):
    pixels = ctf.shape[1]
    parts = images.shape[0]
    rdev = refs.shape[0]
    trans = shifts.shape[0]
    nref = lax.axis_size("ref")
    refs_all = rdev * nref
    me = lax.axis_index("ref")
    cosine, sine = phase_tables(shifts, pixels)
    gain = ctf.astype(jnp.float32)
    weighted = jnp.concatenate(
        [
            gain * images[:, :pixels].astype(jnp.float32),
            gain * images[:, pixels:].astype(jnp.float32),
        ],
        axis=1,
    ).astype(jnp.bfloat16)
    scale = jnp.float32((2 * pixels) ** (-0.5))

    def scored(table, block, column):
        ref_re = block[:, None, :pixels].astype(jnp.float32)
        ref_im = block[:, None, pixels:].astype(jnp.float32)
        rot_re = ref_re * cosine[None] - ref_im * sine[None]
        rot_im = ref_re * sine[None] + ref_im * cosine[None]
        rotated = jnp.concatenate([rot_re, rot_im], axis=2).astype(jnp.bfloat16)
        rotated = rotated.reshape(block.shape[0] * trans, 2 * pixels)
        part_scores = (
            lax.dot_general(
                weighted, rotated, (((1,), (1,)), ((), ())), preferred_element_type=jnp.float32
            )
            * scale
        )
        return lax.dynamic_update_slice_in_dim(table, part_scores, column, 1)

    empty_table = jnp.zeros((parts, refs_all * trans), jnp.float32)

    def one_step(step, carry):
        block, table = carry
        table = scored(table, block, (me - step) % nref * (rdev * trans))
        block = from_behind(block, "ref", 1)
        return (block, table)

    block, table = lax.fori_loop(0, nref - 1, one_step, (refs, empty_table))
    table = scored(table, block, (me - (nref - 1)) % nref * (rdev * trans))
    valid = jnp.arange(lists.shape[1], dtype=jnp.int32)[None, :] < counts[:, None]
    hits = (lists[:, :, None] == jnp.arange(refs_all, dtype=jnp.int32)[None, None, :]) & valid[
        :, :, None
    ]
    listed = jnp.any(hits, axis=1)[:, :, None]
    scores = table.reshape(parts, refs_all, trans)
    masked = jnp.where(listed, scores, -jnp.inf)
    top = jnp.max(masked, axis=(1, 2))
    expd = jnp.where(listed, jnp.exp(masked - top[:, None, None]), jnp.float32(0.0))
    log_evidence = top + jnp.log(jnp.sum(expd, axis=(1, 2)))
    weights = jnp.where(listed, jnp.exp(masked - log_evidence[:, None, None]), jnp.float32(0.0))
    all_totals = lax.psum(jnp.sum(weights, axis=(0, 2)), ("dp", "ref"))
    totals = lax.dynamic_slice_in_dim(all_totals, me * rdev, rdev, 0)
    rounded = weights.astype(jnp.bfloat16).reshape(parts, refs_all * trans)

    def back_rows(start, count):
        columns = lax.dynamic_slice_in_dim(rounded, start * trans, count * trans, 1)
        gathered = lax.dot_general(
            columns, weighted, (((0,), (0,)), ((), ())), preferred_element_type=jnp.float32
        )
        gathered = gathered.reshape(count, trans, 2 * pixels)
        gather_re = gathered[:, :, :pixels]
        gather_im = gathered[:, :, pixels:]
        sums_re = jnp.sum(gather_re * cosine[None] + gather_im * sine[None], axis=1)
        sums_im = jnp.sum(gather_im * cosine[None] - gather_re * sine[None], axis=1)
        return jnp.concatenate([sums_re, sums_im], axis=1)

    def carry_step(step, carried):
        owner = (me - step - 1) % nref
        carried = carried + back_rows(owner * rdev, rdev)
        return from_behind(carried, "ref", 1)

    partial_sums = lax.fori_loop(
        0, nref - 1, carry_step, jnp.zeros((rdev, 2 * pixels), jnp.float32)
    )
    partial_sums = partial_sums + back_rows(me * rdev, rdev)
    sums = lax.psum_scatter(partial_sums, "dp", scatter_dimension=1, tiled=True)
    return (sums, totals, log_evidence)


def solution(mesh):
    placed = (
        P(("dp", "ref"), None),
        P(("dp", "ref"), None),
        P("ref", None),
        P(),
        P(("dp", "ref"), None),
        P(("dp", "ref")),
    )
    return jax.shard_map(
        local,
        mesh=mesh,
        in_specs=placed,
        out_specs=(P("ref", "dp"), P("ref"), P(("dp", "ref"))),
        check_vma=False,
    )
```

profile of v0, /device:TPU:1, one launch (start us, length us, event | category | flops | bytes accessed | tf_op | source)
XLA Modules:
  0.0 1132.9 jit_solution(1994873061769356336)
XLA Ops:
  18.3 313.9 %while.36 = (s32[]{:T(128)}, bf16[12,16384]{1,0:T(8,128)(2,1)}, f32[48,1728]{1,0:T(8,128)S(1)}, bf16[48,16384]{1,0:T(8,128)(2,1)}, s32[]{:T(128)}, /*index=5*/s3...) while((s32[]{:T(128)}, bf16[12,16384]{1,0:T(8,128)(2,1)}, ...), condition=%wide.region_2.3_spmd.clone.clone, body=%wide.region_1.2_spmd.clone.clone.sunk | while | flops 185406528 | bytes 21361824 | solution.py:70
  353.7 10.4 reshape.294
  364.2 7.2 add_reduce_fusion.1
  371.4 657.7 %while.37 = (s32[]{:T(128)}, f32[12,16384]{1,0:T(8,128)S(1)}, s32[]{:T(128)}, bf16[48,1728]{1,0:T(8,128)(2,1)S(1)}, bf16[48,16384]{1,0:T(8,128)(2,1)S(1)}, /*ind...) while((s32[]{:T(128)}, f32[12,16384]{1,0:T(8,128)S(1)}, ...), condition=%wide.region_8.9_spmd.clone.clone, body=%wide.region_5.8_spmd.clone.clone.sunk | while | flops 178323472 | bytes 37433788 | solution.py:104
  371.7 4.1 fusion.79
  375.8 10.4 reshape.298
  389.0 6.3 add_reduce_fusion.3
  396.6 23.5 %collective-permute-done.1 = f32[12,16384]{1,0:T(8,128)S(1)} collective-permute-done((f32[12,16384]{1,0:T(8,128)}, f32[12,16384]{1,0:T(8,128)S(1)}, u32[]{:S(2)}, u32[]{:S(2)}) %collective-permute-start.1) | collective-permute-done | bytes 786464 | tf_op jit(solution)/shard_map/while/body/eval_jaxpr/ppermute | solution.py:14
  420.1 4.1 fusion.79
  424.2 10.4 reshape.298
  437.4 6.3 add_reduce_fusion.3
  444.9 22.7 %collective-permute-done.1 = f32[12,16384]{1,0:T(8,128)S(1)} collective-permute-done((f32[12,16384]{1,0:T(8,128)}, f32[12,16384]{1,0:T(8,128)S(1)}, u32[]{:S(2)}, u32[]{:S(2)}) %collective-permute-start.1) | collective-permute-done | bytes 786464 | tf_op jit(solution)/shard_map/while/body/eval_jaxpr/ppermute | solution.py:14
  467.5 4.1 fusion.79
  471.7 10.4 reshape.298
  484.9 6.3 add_reduce_fusion.3
  492.3 21.8 %collective-permute-done.1 = f32[12,16384]{1,0:T(8,128)S(1)} collective-permute-done((f32[12,16384]{1,0:T(8,128)}, f32[12,16384]{1,0:T(8,128)S(1)}, u32[]{:S(2)}, u32[]{:S(2)}) %collective-permute-start.1) | collective-permute-done | bytes 786464 | tf_op jit(solution)/shard_map/while/body/eval_jaxpr/ppermute | solution.py:14
  514.1 4.1 fusion.79
  518.2 10.4 reshape.298
  531.4 6.3 add_reduce_fusion.3
  538.9 20.8 %collective-permute-done.1 = f32[12,16384]{1,0:T(8,128)S(1)} collective-permute-done((f32[12,16384]{1,0:T(8,128)}, f32[12,16384]{1,0:T(8,128)S(1)}, u32[]{:S(2)}, u32[]{:S(2)}) %collective-permute-start.1) | collective-permute-done | bytes 786464 | tf_op jit(solution)/shard_map/while/body/eval_jaxpr/ppermute | solution.py:14
  559.7 4.1 fusion.79
  563.8 10.4 reshape.298
  577.0 6.3 add_reduce_fusion.3
  584.5 19.9 %collective-permute-done.1 = f32[12,16384]{1,0:T(8,128)S(1)} collective-permute-done((f32[12,16384]{1,0:T(8,128)}, f32[12,16384]{1,0:T(8,128)S(1)}, u32[]{:S(2)}, u32[]{:S(2)}) %collective-permute-start.1) | collective-permute-done | bytes 786464 | tf_op jit(solution)/shard_map/while/body/eval_jaxpr/ppermute | solution.py:14
  604.4 4.1 fusion.79
  608.5 10.4 reshape.298
  621.7 6.3 add_reduce_fusion.3
  629.2 19.0 %collective-permute-done.1 = f32[12,16384]{1,0:T(8,128)S(1)} collective-permute-done((f32[12,16384]{1,0:T(8,128)}, f32[12,16384]{1,0:T(8,128)S(1)}, u32[]{:S(2)}, u32[]{:S(2)}) %collective-permute-start.1) | collective-permute-done | bytes 786464 | tf_op jit(solution)/shard_map/while/body/eval_jaxpr/ppermute | solution.py:14
  648.2 4.1 fusion.79
  652.3 10.4 reshape.298
  665.5 6.3 add_reduce_fusion.3
  673.0 18.1 %collective-permute-done.1 = f32[12,16384]{1,0:T(8,128)S(1)} collective-permute-done((f32[12,16384]{1,0:T(8,128)}, f32[12,16384]{1,0:T(8,128)S(1)}, u32[]{:S(2)}, u32[]{:S(2)}) %collective-permute-start.1) | collective-permute-done | bytes 786464 | tf_op jit(solution)/shard_map/while/body/eval_jaxpr/ppermute | solution.py:14
  691.0 4.1 fusion.79
  695.2 10.4 reshape.298
  708.4 6.3 add_reduce_fusion.3
  715.8 17.5 %collective-permute-done.1 = f32[12,16384]{1,0:T(8,128)S(1)} collective-permute-done((f32[12,16384]{1,0:T(8,128)}, f32[12,16384]{1,0:T(8,128)S(1)}, u32[]{:S(2)}, u32[]{:S(2)}) %collective-permute-start.1) | collective-permute-done | bytes 786464 | tf_op jit(solution)/shard_map/while/body/eval_jaxpr/ppermute | solution.py:14
  733.3 4.1 fusion.79
  737.4 10.4 reshape.298
  750.6 6.3 add_reduce_fusion.3
  758.1 17.5 %collective-permute-done.1 = f32[12,16384]{1,0:T(8,128)S(1)} collective-permute-done((f32[12,16384]{1,0:T(8,128)}, f32[12,16384]{1,0:T(8,128)S(1)}, u32[]{:S(2)}, u32[]{:S(2)}) %collective-permute-start.1) | collective-permute-done | bytes 786464 | tf_op jit(solution)/shard_map/while/body/eval_jaxpr/ppermute | solution.py:14
  775.6 4.1 fusion.79
  779.7 10.4 reshape.298
  792.9 6.3 add_reduce_fusion.3
  800.3 17.5 %collective-permute-done.1 = f32[12,16384]{1,0:T(8,128)S(1)} collective-permute-done((f32[12,16384]{1,0:T(8,128)}, f32[12,16384]{1,0:T(8,128)S(1)}, u32[]{:S(2)}, u32[]{:S(2)}) %collective-permute-start.1) | collective-permute-done | bytes 786464 | tf_op jit(solution)/shard_map/while/body/eval_jaxpr/ppermute | solution.py:14
  817.8 4.1 fusion.79
  822.0 10.4 reshape.298
  835.2 6.3 add_reduce_fusion.3
  842.6 17.5 %collective-permute-done.1 = f32[12,16384]{1,0:T(8,128)S(1)} collective-permute-done((f32[12,16384]{1,0:T(8,128)}, f32[12,16384]{1,0:T(8,128)S(1)}, u32[]{:S(2)}, u32[]{:S(2)}) %collective-permute-start.1) | collective-permute-done | bytes 786464 | tf_op jit(solution)/shard_map/while/body/eval_jaxpr/ppermute | solution.py:14
  860.1 4.1 fusion.79
  864.2 10.4 reshape.298
  877.4 6.3 add_reduce_fusion.3
  884.9 17.5 %collective-permute-done.1 = f32[12,16384]{1,0:T(8,128)S(1)} collective-permute-done((f32[12,16384]{1,0:T(8,128)}, f32[12,16384]{1,0:T(8,128)S(1)}, u32[]{:S(2)}, u32[]{:S(2)}) %collective-permute-start.1) | collective-permute-done | bytes 786464 | tf_op jit(solution)/shard_map/while/body/eval_jaxpr/ppermute | solution.py:14
  902.3 4.1 fusion.79
  906.5 10.4 reshape.298
  919.7 6.3 add_reduce_fusion.3
  927.1 17.5 %collective-permute-done.1 = f32[12,16384]{1,0:T(8,128)S(1)} collective-permute-done((f32[12,16384]{1,0:T(8,128)}, f32[12,16384]{1,0:T(8,128)S(1)}, u32[]{:S(2)}, u32[]{:S(2)}) %collective-permute-start.1) | collective-permute-done | bytes 786464 | tf_op jit(solution)/shard_map/while/body/eval_jaxpr/ppermute | solution.py:14
  948.7 10.4 reshape.298
  961.9 6.3 add_reduce_fusion.3
  969.4 17.5 %collective-permute-done.1 = f32[12,16384]{1,0:T(8,128)S(1)} collective-permute-done((f32[12,16384]{1,0:T(8,128)}, f32[12,16384]{1,0:T(8,128)S(1)}, u32[]{:S(2)}, u32[]{:S(2)}) %collective-permute-start.1) | collective-permute-done | bytes 786464 | tf_op jit(solution)/shard_map/while/body/eval_jaxpr/ppermute | solution.py:14
  986.9 4.1 fusion.79
  991.0 10.4 reshape.298
  1004.2 6.3 add_reduce_fusion.3
  1011.6 17.5 %collective-permute-done.1 = f32[12,16384]{1,0:T(8,128)S(1)} collective-permute-done((f32[12,16384]{1,0:T(8,128)}, f32[12,16384]{1,0:T(8,128)S(1)}, u32[]{:S(2)}, u32[]{:S(2)}) %collective-permute-start.1) | collective-permute-done | bytes 786464 | tf_op jit(solution)/shard_map/while/body/eval_jaxpr/ppermute | solution.py:14
  1031.6 93.9 %psum.7 = f32[192]{0:T(256)S(1)} all-reduce(f32[192]{0:T(256)S(1)} %reduce_sum.80), channel_id=1, replica_groups=mesh['dp'=16,'ref'=16] {'dp','ref'}, use_global_device_ids=true, to_apply=%region_14.15 | all-reduce | flops 192 | bytes 1536 | tf_op jit(solution)/shard_map/psum | solution.py:83
  (250 shorter events, 412.6 us)
Async XLA Ops:
  7.2 1118.9 %reduce-scatter.2.cloned.1.call-start = ((), (), s32[]{:S(2)}) async-start(), calls=%async_computation.1 | async-start | bytes 1114112 | tf_op jit(solution)/shard_map/reduce_scatter | solution.py:108
  12.4 0.9 copy-start.1
  12.4 2.1 copy-start.3
  20.2 21.0 %collective-permute-start = (bf16[12,16384]{1,0:T(8,128)(2,1)}, bf16[12,16384]{1,0:T(8,128)(2,1)}, u32[]{:S(2)}, u32[]{:S(2)}) collective-permute-start(bf16[12,16384]{1,0:T(8,128)(2,1)} %copy.30), channel_id=1, source_target_pairs={{0,1},{1,2},{2,3},{3,4},{4,5},{5,6},{6,7},{7,8},{8,9},{9,10},{10,1... | collective-permute-start | bytes 1179656 | tf_op jit(solution)/shard_map/while/body/eval_jaxpr/ppermute | solution.py:14
  43.1 17.9 %collective-permute-start = (bf16[12,16384]{1,0:T(8,128)(2,1)}, bf16[12,16384]{1,0:T(8,128)(2,1)}, u32[]{:S(2)}, u32[]{:S(2)}) collective-permute-start(bf16[12,16384]{1,0:T(8,128)(2,1)} %copy.30), channel_id=1, source_target_pairs={{0,1},{1,2},{2,3},{3,4},{4,5},{5,6},{6,7},{7,8},{8,9},{9,10},{10,1... | collective-permute-start | bytes 1179656 | tf_op jit(solution)/shard_map/while/body/eval_jaxpr/ppermute | solution.py:14
  62.9 19.6 %collective-permute-start = (bf16[12,16384]{1,0:T(8,128)(2,1)}, bf16[12,16384]{1,0:T(8,128)(2,1)}, u32[]{:S(2)}, u32[]{:S(2)}) collective-permute-start(bf16[12,16384]{1,0:T(8,128)(2,1)} %copy.30), channel_id=1, source_target_pairs={{0,1},{1,2},{2,3},{3,4},{4,5},{5,6},{6,7},{7,8},{8,9},{9,10},{10,1... | collective-permute-start | bytes 1179656 | tf_op jit(solution)/shard_map/while/body/eval_jaxpr/ppermute | solution.py:14
  84.5 18.4 %collective-permute-start = (bf16[12,16384]{1,0:T(8,128)(2,1)}, bf16[12,16384]{1,0:T(8,128)(2,1)}, u32[]{:S(2)}, u32[]{:S(2)}) collective-permute-start(bf16[12,16384]{1,0:T(8,128)(2,1)} %copy.30), channel_id=1, source_target_pairs={{0,1},{1,2},{2,3},{3,4},{4,5},{5,6},{6,7},{7,8},{8,9},{9,10},{10,1... | collective-permute-start | bytes 1179656 | tf_op jit(solution)/shard_map/while/body/eval_jaxpr/ppermute | solution.py:14
  104.8 19.6 %collective-permute-start = (bf16[12,16384]{1,0:T(8,128)(2,1)}, bf16[12,16384]{1,0:T(8,128)(2,1)}, u32[]{:S(2)}, u32[]{:S(2)}) collective-permute-start(bf16[12,16384]{1,0:T(8,128)(2,1)} %copy.30), channel_id=1, source_target_pairs={{0,1},{1,2},{2,3},{3,4},{4,5},{5,6},{6,7},{7,8},{8,9},{9,10},{10,1... | collective-permute-start | bytes 1179656 | tf_op jit(solution)/shard_map/while/body/eval_jaxpr/ppermute | solution.py:14
  126.3 18.4 %collective-permute-start = (bf16[12,16384]{1,0:T(8,128)(2,1)}, bf16[12,16384]{1,0:T(8,128)(2,1)}, u32[]{:S(2)}, u32[]{:S(2)}) collective-permute-start(bf16[12,16384]{1,0:T(8,128)(2,1)} %copy.30), channel_id=1, source_target_pairs={{0,1},{1,2},{2,3},{3,4},{4,5},{5,6},{6,7},{7,8},{8,9},{9,10},{10,1... | collective-permute-start | bytes 1179656 | tf_op jit(solution)/shard_map/while/body/eval_jaxpr/ppermute | solution.py:14
  146.6 19.6 %collective-permute-start = (bf16[12,16384]{1,0:T(8,128)(2,1)}, bf16[12,16384]{1,0:T(8,128)(2,1)}, u32[]{:S(2)}, u32[]{:S(2)}) collective-permute-start(bf16[12,16384]{1,0:T(8,128)(2,1)} %copy.30), channel_id=1, source_target_pairs={{0,1},{1,2},{2,3},{3,4},{4,5},{5,6},{6,7},{7,8},{8,9},{9,10},{10,1... | collective-permute-start | bytes 1179656 | tf_op jit(solution)/shard_map/while/body/eval_jaxpr/ppermute | solution.py:14
  168.2 19.6 %collective-permute-start = (bf16[12,16384]{1,0:T(8,128)(2,1)}, bf16[12,16384]{1,0:T(8,128)(2,1)}, u32[]{:S(2)}, u32[]{:S(2)}) collective-permute-start(bf16[12,16384]{1,0:T(8,128)(2,1)} %copy.30), channel_id=1, source_target_pairs={{0,1},{1,2},{2,3},{3,4},{4,5},{5,6},{6,7},{7,8},{8,9},{9,10},{10,1... | collective-permute-start | bytes 1179656 | tf_op jit(solution)/shard_map/while/body/eval_jaxpr/ppermute | solution.py:14
  189.7 19.6 %collective-permute-start = (bf16[12,16384]{1,0:T(8,128)(2,1)}, bf16[12,16384]{1,0:T(8,128)(2,1)}, u32[]{:S(2)}, u32[]{:S(2)}) collective-permute-start(bf16[12,16384]{1,0:T(8,128)(2,1)} %copy.30), channel_id=1, source_target_pairs={{0,1},{1,2},{2,3},{3,4},{4,5},{5,6},{6,7},{7,8},{8,9},{9,10},{10,1... | collective-permute-start | bytes 1179656 | tf_op jit(solution)/shard_map/while/body/eval_jaxpr/ppermute | solution.py:14
  211.2 17.5 %collective-permute-start = (bf16[12,16384]{1,0:T(8,128)(2,1)}, bf16[12,16384]{1,0:T(8,128)(2,1)}, u32[]{:S(2)}, u32[]{:S(2)}) collective-permute-start(bf16[12,16384]{1,0:T(8,128)(2,1)} %copy.30), channel_id=1, source_target_pairs={{0,1},{1,2},{2,3},{3,4},{4,5},{5,6},{6,7},{7,8},{8,9},{9,10},{10,1... | collective-permute-start | bytes 1179656 | tf_op jit(solution)/shard_map/while/body/eval_jaxpr/ppermute | solution.py:14
  230.7 19.6 %collective-permute-start = (bf16[12,16384]{1,0:T(8,128)(2,1)}, bf16[12,16384]{1,0:T(8,128)(2,1)}, u32[]{:S(2)}, u32[]{:S(2)}) collective-permute-start(bf16[12,16384]{1,0:T(8,128)(2,1)} %copy.30), channel_id=1, source_target_pairs={{0,1},{1,2},{2,3},{3,4},{4,5},{5,6},{6,7},{7,8},{8,9},{9,10},{10,1... | collective-permute-start | bytes 1179656 | tf_op jit(solution)/shard_map/while/body/eval_jaxpr/ppermute | solution.py:14
  252.2 17.5 %collective-permute-start = (bf16[12,16384]{1,0:T(8,128)(2,1)}, bf16[12,16384]{1,0:T(8,128)(2,1)}, u32[]{:S(2)}, u32[]{:S(2)}) collective-permute-start(bf16[12,16384]{1,0:T(8,128)(2,1)} %copy.30), channel_id=1, source_target_pairs={{0,1},{1,2},{2,3},{3,4},{4,5},{5,6},{6,7},{7,8},{8,9},{9,10},{10,1... | collective-permute-start | bytes 1179656 | tf_op jit(solution)/shard_map/while/body/eval_jaxpr/ppermute | solution.py:14
  271.6 19.6 %collective-permute-start = (bf16[12,16384]{1,0:T(8,128)(2,1)}, bf16[12,16384]{1,0:T(8,128)(2,1)}, u32[]{:S(2)}, u32[]{:S(2)}) collective-permute-start(bf16[12,16384]{1,0:T(8,128)(2,1)} %copy.30), channel_id=1, source_target_pairs={{0,1},{1,2},{2,3},{3,4},{4,5},{5,6},{6,7},{7,8},{8,9},{9,10},{10,1... | collective-permute-start | bytes 1179656 | tf_op jit(solution)/shard_map/while/body/eval_jaxpr/ppermute | solution.py:14
  293.2 17.5 %collective-permute-start = (bf16[12,16384]{1,0:T(8,128)(2,1)}, bf16[12,16384]{1,0:T(8,128)(2,1)}, u32[]{:S(2)}, u32[]{:S(2)}) collective-permute-start(bf16[12,16384]{1,0:T(8,128)(2,1)} %copy.30), channel_id=1, source_target_pairs={{0,1},{1,2},{2,3},{3,4},{4,5},{5,6},{6,7},{7,8},{8,9},{9,10},{10,1... | collective-permute-start | bytes 1179656 | tf_op jit(solution)/shard_map/while/body/eval_jaxpr/ppermute | solution.py:14
  312.6 19.6 %collective-permute-start = (bf16[12,16384]{1,0:T(8,128)(2,1)}, bf16[12,16384]{1,0:T(8,128)(2,1)}, u32[]{:S(2)}, u32[]{:S(2)}) collective-permute-start(bf16[12,16384]{1,0:T(8,128)(2,1)} %copy.30), channel_id=1, source_target_pairs={{0,1},{1,2},{2,3},{3,4},{4,5},{5,6},{6,7},{7,8},{8,9},{9,10},{10,1... | collective-permute-start | bytes 1179656 | tf_op jit(solution)/shard_map/while/body/eval_jaxpr/ppermute | solution.py:14
  342.7 4.4 copy-start.9
  342.7 4.5 copy-start.7
  346.7 3.0 copy-start.2
  346.7 3.0 copy-start.4
  349.1 4.6 copy-start.8
  353.7 10.5 copy-start.5
  353.7 10.5 copy-start.6
  364.2 7.2 copy-start
  396.5 23.6 %collective-permute-start.1 = (f32[12,16384]{1,0:T(8,128)}, f32[12,16384]{1,0:T(8,128)S(1)}, u32[]{:S(2)}, u32[]{:S(2)}) collective-permute-start(f32[12,16384]{1,0:T(8,128)} %maximum_add_fusion.3), channel_id=1, source_target_pairs={{0,1},{1,2},{2,3},{3,4},{4,5},{5,6},{6,7},{7,8},{8,9},{9,10},{10,1... | collective-permute-start | bytes 2359304 | tf_op jit(solution)/shard_map/while/body/eval_jaxpr/ppermute | solution.py:14
  444.9 22.7 %collective-permute-start.1 = (f32[12,16384]{1,0:T(8,128)}, f32[12,16384]{1,0:T(8,128)S(1)}, u32[]{:S(2)}, u32[]{:S(2)}) collective-permute-start(f32[12,16384]{1,0:T(8,128)} %maximum_add_fusion.3), channel_id=1, source_target_pairs={{0,1},{1,2},{2,3},{3,4},{4,5},{5,6},{6,7},{7,8},{8,9},{9,10},{10,1... | collective-permute-start | bytes 2359304 | tf_op jit(solution)/shard_map/while/body/eval_jaxpr/ppermute | solution.py:14
  492.3 21.8 %collective-permute-start.1 = (f32[12,16384]{1,0:T(8,128)}, f32[12,16384]{1,0:T(8,128)S(1)}, u32[]{:S(2)}, u32[]{:S(2)}) collective-permute-start(f32[12,16384]{1,0:T(8,128)} %maximum_add_fusion.3), channel_id=1, source_target_pairs={{0,1},{1,2},{2,3},{3,4},{4,5},{5,6},{6,7},{7,8},{8,9},{9,10},{10,1... | collective-permute-start | bytes 2359304 | tf_op jit(solution)/shard_map/while/body/eval_jaxpr/ppermute | solution.py:14
  538.9 20.8 %collective-permute-start.1 = (f32[12,16384]{1,0:T(8,128)}, f32[12,16384]{1,0:T(8,128)S(1)}, u32[]{:S(2)}, u32[]{:S(2)}) collective-permute-start(f32[12,16384]{1,0:T(8,128)} %maximum_add_fusion.3), channel_id=1, source_target_pairs={{0,1},{1,2},{2,3},{3,4},{4,5},{5,6},{6,7},{7,8},{8,9},{9,10},{10,1... | collective-permute-start | bytes 2359304 | tf_op jit(solution)/shard_map/while/body/eval_jaxpr/ppermute | solution.py:14
  584.5 19.9 %collective-permute-start.1 = (f32[12,16384]{1,0:T(8,128)}, f32[12,16384]{1,0:T(8,128)S(1)}, u32[]{:S(2)}, u32[]{:S(2)}) collective-permute-start(f32[12,16384]{1,0:T(8,128)} %maximum_add_fusion.3), channel_id=1, source_target_pairs={{0,1},{1,2},{2,3},{3,4},{4,5},{5,6},{6,7},{7,8},{8,9},{9,10},{10,1... | collective-permute-start | bytes 2359304 | tf_op jit(solution)/shard_map/while/body/eval_jaxpr/ppermute | solution.py:14
  629.2 19.0 %collective-permute-start.1 = (f32[12,16384]{1,0:T(8,128)}, f32[12,16384]{1,0:T(8,128)S(1)}, u32[]{:S(2)}, u32[]{:S(2)}) collective-permute-start(f32[12,16384]{1,0:T(8,128)} %maximum_add_fusion.3), channel_id=1, source_target_pairs={{0,1},{1,2},{2,3},{3,4},{4,5},{5,6},{6,7},{7,8},{8,9},{9,10},{10,1... | collective-permute-start | bytes 2359304 | tf_op jit(solution)/shard_map/while/body/eval_jaxpr/ppermute | solution.py:14
  673.0 18.1 %collective-permute-start.1 = (f32[12,16384]{1,0:T(8,128)}, f32[12,16384]{1,0:T(8,128)S(1)}, u32[]{:S(2)}, u32[]{:S(2)}) collective-permute-start(f32[12,16384]{1,0:T(8,128)} %maximum_add_fusion.3), channel_id=1, source_target_pairs={{0,1},{1,2},{2,3},{3,4},{4,5},{5,6},{6,7},{7,8},{8,9},{9,10},{10,1... | collective-permute-start | bytes 2359304 | tf_op jit(solution)/shard_map/while/body/eval_jaxpr/ppermute | solution.py:14
  715.8 17.5 %collective-permute-start.1 = (f32[12,16384]{1,0:T(8,128)}, f32[12,16384]{1,0:T(8,128)S(1)}, u32[]{:S(2)}, u32[]{:S(2)}) collective-permute-start(f32[12,16384]{1,0:T(8,128)} %maximum_add_fusion.3), channel_id=1, source_target_pairs={{0,1},{1,2},{2,3},{3,4},{4,5},{5,6},{6,7},{7,8},{8,9},{9,10},{10,1... | collective-permute-start | bytes 2359304 | tf_op jit(solution)/shard_map/while/body/eval_jaxpr/ppermute | solution.py:14
  758.1 17.5 %collective-permute-start.1 = (f32[12,16384]{1,0:T(8,128)}, f32[12,16384]{1,0:T(8,128)S(1)}, u32[]{:S(2)}, u32[]{:S(2)}) collective-permute-start(f32[12,16384]{1,0:T(8,128)} %maximum_add_fusion.3), channel_id=1, source_target_pairs={{0,1},{1,2},{2,3},{3,4},{4,5},{5,6},{6,7},{7,8},{8,9},{9,10},{10,1... | collective-permute-start | bytes 2359304 | tf_op jit(solution)/shard_map/while/body/eval_jaxpr/ppermute | solution.py:14
  800.3 17.5 %collective-permute-start.1 = (f32[12,16384]{1,0:T(8,128)}, f32[12,16384]{1,0:T(8,128)S(1)}, u32[]{:S(2)}, u32[]{:S(2)}) collective-permute-start(f32[12,16384]{1,0:T(8,128)} %maximum_add_fusion.3), channel_id=1, source_target_pairs={{0,1},{1,2},{2,3},{3,4},{4,5},{5,6},{6,7},{7,8},{8,9},{9,10},{10,1... | collective-permute-start | bytes 2359304 | tf_op jit(solution)/shard_map/while/body/eval_jaxpr/ppermute | solution.py:14
  842.6 17.5 %collective-permute-start.1 = (f32[12,16384]{1,0:T(8,128)}, f32[12,16384]{1,0:T(8,128)S(1)}, u32[]{:S(2)}, u32[]{:S(2)}) collective-permute-start(f32[12,16384]{1,0:T(8,128)} %maximum_add_fusion.3), channel_id=1, source_target_pairs={{0,1},{1,2},{2,3},{3,4},{4,5},{5,6},{6,7},{7,8},{8,9},{9,10},{10,1... | collective-permute-start | bytes 2359304 | tf_op jit(solution)/shard_map/while/body/eval_jaxpr/ppermute | solution.py:14
  884.9 17.5 %collective-permute-start.1 = (f32[12,16384]{1,0:T(8,128)}, f32[12,16384]{1,0:T(8,128)S(1)}, u32[]{:S(2)}, u32[]{:S(2)}) collective-permute-start(f32[12,16384]{1,0:T(8,128)} %maximum_add_fusion.3), channel_id=1, source_target_pairs={{0,1},{1,2},{2,3},{3,4},{4,5},{5,6},{6,7},{7,8},{8,9},{9,10},{10,1... | collective-permute-start | bytes 2359304 | tf_op jit(solution)/shard_map/while/body/eval_jaxpr/ppermute | solution.py:14
  927.1 17.5 %collective-permute-start.1 = (f32[12,16384]{1,0:T(8,128)}, f32[12,16384]{1,0:T(8,128)S(1)}, u32[]{:S(2)}, u32[]{:S(2)}) collective-permute-start(f32[12,16384]{1,0:T(8,128)} %maximum_add_fusion.3), channel_id=1, source_target_pairs={{0,1},{1,2},{2,3},{3,4},{4,5},{5,6},{6,7},{7,8},{8,9},{9,10},{10,1... | collective-permute-start | bytes 2359304 | tf_op jit(solution)/shard_map/while/body/eval_jaxpr/ppermute | solution.py:14
  969.4 17.5 %collective-permute-start.1 = (f32[12,16384]{1,0:T(8,128)}, f32[12,16384]{1,0:T(8,128)S(1)}, u32[]{:S(2)}, u32[]{:S(2)}) collective-permute-start(f32[12,16384]{1,0:T(8,128)} %maximum_add_fusion.3), channel_id=1, source_target_pairs={{0,1},{1,2},{2,3},{3,4},{4,5},{5,6},{6,7},{7,8},{8,9},{9,10},{10,1... | collective-permute-start | bytes 2359304 | tf_op jit(solution)/shard_map/while/body/eval_jaxpr/ppermute | solution.py:14
  1011.6 17.5 %collective-permute-start.1 = (f32[12,16384]{1,0:T(8,128)}, f32[12,16384]{1,0:T(8,128)S(1)}, u32[]{:S(2)}, u32[]{:S(2)}) collective-permute-start(f32[12,16384]{1,0:T(8,128)} %maximum_add_fusion.3), channel_id=1, source_target_pairs={{0,1},{1,2},{2,3},{3,4},{4,5},{5,6},{6,7},{7,8},{8,9},{9,10},{10,1... | collective-permute-start | bytes 2359304 | tf_op jit(solution)/shard_map/while/body/eval_jaxpr/ppermute | solution.py:14
Sparse Core Ops, SparseCore 0:
  1031.4 75.0 reduce-scatter.1
where the time goes:
time: 1140 us; the launch traced here: 1130 us
  local copies, waits for them, and re-layouts  297 us (26%)
  waiting for transfers between devices  286 us (25%)
  other arithmetic  280 us (25%)
  matrix products  129 us (11%)
  blocking collectives  93.9 us (8%)
  starting transfers between devices  32.2 us (3%)
  between operations  14.2 us (1%)
    ppermute x30, waiting for transfers between devices, from_behind(): return lax.ppermute(value, axis, pairs)  286 us
    reshape x16, local copies, waits for them, and re-layouts, back_rows(): gathered = gathered.reshape(count, trans, 2 * pixels)  166 us
    reduce_sum x16, other arithmetic, back_rows(): sums_re = jnp.sum(gather_re * cosine[None] + gather_im * sine[None], axis=1)  102 us
    psum x1, blocking collectives, local(): all_totals = lax.psum(jnp.sum(weights, axis=(0, 2)), ('dp', 'ref'))  93.9 us
    cos x31, other arithmetic, phase_tables(): return (jnp.cos(angle), jnp.sin(angle))  89 us
    dot_general x16, matrix products, back_rows(): lax.dot_general(columns, weighted, (((0,), (0,)), ((), ())), preferred_el...  66.1 us
    dot_general x16, matrix products, scored(): lax.dot_general(weighted, rotated, (((1,), (1,)), ((), ())), preferred_el...  62.9 us
    add x16, local copies, waits for them, and re-layouts, scored(): rot_im = ref_re * sine[None] + ref_im * cosine[None]  54.5 us
  transfers between devices with their start and end apart: 31, of which 16 were waited for; matrix products, arithmetic and copies ran while one was open for 22% of the time, Pallas kernels for 0%

commit v1 on v0

v1 whole, which is shorter than its diff:
```python
import math

import jax
import jax.numpy as jnp
from jax import lax
from jax.experimental import pallas as pl
from jax.experimental.pallas import tpu as pltpu
from jax.sharding import Mesh, PartitionSpec as P

GRID = 128
BLOCK = 1024
LANES = 128
GROUPS = BLOCK // LANES
CHUNK = 256
CHIPS = ("z", "y_hi", "y_lo", "x")
EVERYONE = ("y_lo", "x", "core", "z", "y_hi")
SMEM = pl.BlockSpec(memory_space=pltpu.SMEM)
VMEM = pl.BlockSpec(memory_space=pltpu.VMEM)


def pack_kernel(column_ref, odd_ref, refs_ref, out_ref):
    column = pl.multiple_of(column_ref[0] * BLOCK, BLOCK)
    odd = odd_ref[0] == 1
    block = refs_ref[:, pl.ds(column, BLOCK)].astype(jnp.float32)
    whole = jnp.where(odd, block[4:12], block[0:8])
    rest = jnp.where(odd, block[0:4], block[8:12])
    tiles = [whole[:, g * LANES : (g + 1) * LANES] for g in range(GROUPS)]
    tiles += [rest[:, g * LANES : (g + 1) * LANES] for g in range(GROUPS)]
    out_ref[...] = jnp.concatenate(tiles, axis=0).astype(jnp.bfloat16)


def unpack_kernel(odd_ref, flat_ref, out_ref):
    odd = odd_ref[0] == 1
    for g in range(GROUPS):
        lanes = slice(g * LANES, (g + 1) * LANES)
        whole = flat_ref[8 * g : 8 * g + 8]
        rest = flat_ref[8 * GROUPS + 4 * g : 8 * GROUPS + 4 * g + 4]
        block = jnp.where(
            odd,
            jnp.concatenate([rest, whole], axis=0),
            jnp.concatenate([whole, rest], axis=0),
        )
        out_ref[:, lanes] = block


def weighted_kernel(core_ref, images_ref, ctf_ref, own_ref, other_ref):
    core = core_ref[0]
    pairs = own_ref.shape[0] // 2
    for out_ref, half in ((own_ref, core), (other_ref, 1 - core)):
        for pair in range(pairs):
            column = pl.multiple_of((2 * pair + half) * BLOCK, BLOCK)
            gain = ctf_ref[:, pl.ds(column, BLOCK)].astype(jnp.float32)
            for part in range(2):
                start = pl.multiple_of(part * 2 * pairs * BLOCK + column, BLOCK)
                values = images_ref[:, pl.ds(start, BLOCK)].astype(jnp.float32)
                out_ref[part * pairs + pair] = (gain * values).astype(jnp.bfloat16)


def rotate_kernel(core_ref, shifts_ref, own_ref, recv_ref, rot_ref, cos_ref, sin_ref):
    core = core_ref[0]
    pairs, rows = own_ref.shape[0] // 2, own_ref.shape[1]
    trans = shifts_ref.shape[0]
    half = GRID // 2
    steps = BLOCK // CHUNK

    def step(index, carry):
        pair = index // steps
        start = pl.multiple_of((index % steps) * CHUNK, CHUNK)
        lanes = pl.ds(start, CHUNK)
        pixel = (2 * pair + core) * BLOCK + start
        pixel = pixel + lax.broadcasted_iota(jnp.int32, (trans, CHUNK), 1)
        freq_y = (((pixel >> 6) + half) & (GRID - 1)) - half
        turns = (pixel & (half - 1)) * shifts_ref[:, 0:1] + freq_y * shifts_ref[:, 1:2]
        angle = (turns & (GRID - 1)).astype(jnp.float32) * jnp.float32(2.0 * math.pi / GRID)
        cos_ref[...] = jnp.cos(angle)
        sin_ref[...] = jnp.sin(angle)
        for h, half_ref in enumerate((own_ref, recv_ref)):
            re = half_ref[pair, :, lanes].astype(jnp.float32)
            im = half_ref[pairs + pair, :, lanes].astype(jnp.float32)
            for t in range(trans):
                cosine, sine = cos_ref[t : t + 1, :], sin_ref[t : t + 1, :]
                base = (h * trans + t) * rows
                rot_ref[pair, base : base + rows, lanes] = (re * cosine + im * sine).astype(
                    jnp.bfloat16
                )
                rot_ref[pairs + pair, base : base + rows, lanes] = (im * cosine - re * sine).astype(
                    jnp.bfloat16
                )
        return carry

    lax.fori_loop(0, pairs * steps, step, 0)


def spread_piece(flat_ref, wide_ref, piece):
    low = lax.broadcasted_iota(jnp.int32, (8, LANES), 0) < 4
    for two in range(flat_ref.shape[0] // 2):
        even = flat_ref[2 * two, piece].astype(jnp.float32)
        odd = flat_ref[2 * two + 1, piece].astype(jnp.float32)
        row = 24 * two
        for g in range(GROUPS):
            lanes = slice(g * LANES, (g + 1) * LANES)
            wide_ref[row : row + 8, lanes] = even[8 * g : 8 * g + 8]
            wide_ref[row + 16 : row + 24, lanes] = odd[8 * g : 8 * g + 8]
        for j in range(GROUPS // 2):
            at = 8 * (GROUPS + j)
            a, b = even[at : at + 8], odd[at : at + 8]
            lanes = slice(2 * j * LANES, (2 * j + 1) * LANES)
            wide_ref[row + 8 : row + 16, lanes] = jnp.where(low, a, pltpu.roll(b, 4, 0))
            lanes = slice((2 * j + 1) * LANES, (2 * j + 2) * LANES)
            wide_ref[row + 8 : row + 16, lanes] = jnp.where(low, pltpu.roll(a, 4, 0), b)
    return wide_ref[...].astype(jnp.bfloat16)


def forward_kernel(flat_ref, rot_ref, out_ref, wide_ref):
    pairs = rot_ref.shape[0] // 2
    for pair in range(pairs):
        total = None
        for part in range(2):
            piece = part * pairs + pair
            product = lax.dot_general(
                rot_ref[piece],
                spread_piece(flat_ref, wide_ref.at[part], piece),
                (((1,), (1,)), ((), ())),
                preferred_element_type=jnp.float32,
            )
            total = product if total is None else total + product
        count = total.shape[1]
        if pair == 0:
            out_ref[:, :count] = total
            out_ref[:, count:] = jnp.zeros((total.shape[0], out_ref.shape[1] - count), jnp.float32)
        else:
            out_ref[:, :count] += total


def softmax(scale, mine_ref, theirs_ref, lists_ref, weights_ref, evidence_ref, totals_ref):
    particles, slots = lists_ref.shape[1:]
    refs_all = weights_ref.shape[1]
    trans = mine_ref.shape[0] // (2 * particles)
    index = lax.broadcasted_iota(jnp.int32, (particles, refs_all), 1)
    for h in range(2):
        listed = index == lists_ref[h, :, 0:1]
        for k in range(1, slots):
            listed = listed | (index == lists_ref[h, :, k : k + 1])
        scores = []
        for t in range(trans):
            a = (h * trans + t) * particles
            b = ((1 - h) * trans + t) * particles
            value = mine_ref[a : a + particles, :refs_all] + theirs_ref[b : b + particles, :refs_all]
            scores.append(jnp.where(listed, value * scale, -jnp.inf))
        top = scores[0]
        for value in scores[1:]:
            top = jnp.maximum(top, value)
        top = jnp.max(top, axis=1, keepdims=True)
        exps = [jnp.exp(value - top) for value in scores]
        norm = exps[0]
        for value in exps[1:]:
            norm = norm + value
        summed = jnp.sum(norm, axis=1, keepdims=True)
        inverse = 1.0 / summed
        for t in range(trans):
            a = (h * trans + t) * particles
            weights_ref[a : a + particles] = exps[t] * inverse
        if h == 0:
            evidence_ref[...] = top + jnp.log(summed)
            totals_ref[...] = jnp.sum(norm * inverse, axis=0, keepdims=True)


def backward_kernel(
    scale,
    mine_ref,
    theirs_ref,
    lists_ref,
    rot_ref,
    out_ref,
    evidence_ref,
    totals_ref,
    weights_ref,
    flat_ref,
    sems,
):
    softmax(scale, mine_ref, theirs_ref, lists_ref, weights_ref, evidence_ref, totals_ref)
    flipped = weights_ref[...].T.astype(jnp.bfloat16)
    low = lax.broadcasted_iota(jnp.int32, (8, LANES), 0) < 4
    copies = []
    for piece in range(rot_ref.shape[0]):
        product = lax.dot_general(
            flipped, rot_ref[piece], (((1,), (0,)), ((), ())), preferred_element_type=jnp.float32
        )
        for two in range(flat_ref.shape[1] // 2):
            row = 24 * two
            for g in range(GROUPS):
                lanes = slice(g * LANES, (g + 1) * LANES)
                flat_ref[piece, 2 * two, 8 * g : 8 * g + 8] = product[row : row + 8, lanes]
                flat_ref[piece, 2 * two + 1, 8 * g : 8 * g + 8] = product[row + 16 : row + 24, lanes]
            for j in range(GROUPS // 2):
                at = 8 * (GROUPS + j)
                a = product[row + 8 : row + 16, 2 * j * LANES : (2 * j + 1) * LANES]
                b = product[row + 8 : row + 16, (2 * j + 1) * LANES : (2 * j + 2) * LANES]
                flat_ref[piece, 2 * two, at : at + 8] = jnp.where(low, a, pltpu.roll(b, 4, 0))
                flat_ref[piece, 2 * two + 1, at : at + 8] = jnp.where(low, pltpu.roll(a, 4, 0), b)
        copy = pltpu.make_async_copy(flat_ref.at[piece], out_ref.at[:, piece], sems.at[piece])
        copy.start()
        copies.append(copy)
    for copy in copies:
        copy.wait()


def everyones_sum(value):
    for axis in ("core", "y_lo", "y_hi", "x", "z"):
        count = lax.axis_size(axis)
        bit = 1
        while bit < count:
            value = value + lax.ppermute(value, axis, [(i, i ^ bit) for i in range(count)])
            bit *= 2
    return value


def params(mebibytes):
    return pltpu.CompilerParams(vmem_limit_bytes=mebibytes * 1024 * 1024)


def local(images, ctf, refs, shifts, lists, counts):
    parts = images.shape[0]
    rdev = refs.shape[0]
    trans = shifts.shape[0]
    nref = lax.axis_size("z") * lax.axis_size("y_hi")
    pieces = lax.axis_size("y_lo") * lax.axis_size("x")
    refs_all = rdev * nref
    rows = 2 * trans * parts
    swap = [(0, 1), (1, 0)]
    core = lax.axis_index("core")
    column = jnp.full((1,), lax.axis_index(("y_lo", "x")) * 2 + core, jnp.int32)
    odd = jnp.full((1,), lax.axis_index("y_hi"), jnp.int32)
    core = jnp.full((1,), core, jnp.int32)

    mine = pl.pallas_call(
        pack_kernel,
        out_shape=jax.ShapeDtypeStruct((rdev * GROUPS, LANES), jnp.bfloat16),
        in_specs=[SMEM, SMEM, VMEM],
        out_specs=VMEM,
        name="pack",
    )(column, odd, refs)
    gathered = lax.all_gather(mine, CHIPS, axis=0, tiled=True)
    gathered = gathered.reshape(nref, pieces, rdev * GROUPS, LANES)

    half = jax.ShapeDtypeStruct((pieces, parts, BLOCK), jnp.bfloat16)
    own, other = pl.pallas_call(
        weighted_kernel,
        out_shape=(half, half),
        in_specs=[SMEM, VMEM, VMEM],
        out_specs=(VMEM, VMEM),
        compiler_params=params(16),
        name="weighted",
    )(core, images, ctf)
    recv = lax.ppermute(other, "core", swap)
    slot = jnp.arange(lists.shape[1], dtype=jnp.int32)[None, :]
    used = jnp.where(slot < counts[:, None], lists, -1)
    used_pair = jnp.stack([used, lax.ppermute(used, "core", swap)])

    rot = pl.pallas_call(
        rotate_kernel,
        out_shape=jax.ShapeDtypeStruct((pieces, rows, BLOCK), jnp.bfloat16),
        in_specs=[SMEM, VMEM, VMEM, VMEM],
        out_specs=VMEM,
        scratch_shapes=[pltpu.VMEM((trans, CHUNK), jnp.float32)] * 2,
        compiler_params=params(16),
        name="rotate",
    )(core, shifts, own, recv)

    scores = pl.pallas_call(
        forward_kernel,
        out_shape=jax.ShapeDtypeStruct((rows, -(-refs_all // LANES) * LANES), jnp.float32),
        in_specs=[VMEM, VMEM],
        out_specs=VMEM,
        scratch_shapes=[pltpu.VMEM((2, refs_all, BLOCK), jnp.float32)],
        compiler_params=params(16),
        name="forward",
    )(gathered, rot)
    theirs = lax.ppermute(scores, "core", swap)

    scale = (2 * ctf.shape[1]) ** -0.5
    partial, evidence, totals = pl.pallas_call(
        lambda *args: backward_kernel(scale, *args),
        out_shape=(
            jax.ShapeDtypeStruct((nref, pieces, rdev * GROUPS, LANES), jnp.float32),
            jax.ShapeDtypeStruct((parts, 1), jnp.float32),
            jax.ShapeDtypeStruct((1, refs_all), jnp.float32),
        ),
        in_specs=[VMEM, VMEM, VMEM, VMEM],
        out_specs=(pl.BlockSpec(memory_space=pl.ANY), VMEM, VMEM),
        scratch_shapes=[
            pltpu.VMEM((rows, refs_all), jnp.float32),
            pltpu.VMEM((pieces, nref, rdev * GROUPS, LANES), jnp.float32),
            pltpu.SemaphoreType.DMA((pieces,)),
        ],
        compiler_params=params(20),
        name="backward",
    )(scores, theirs, used_pair, rot)

    partial = partial.reshape(nref * pieces * rdev * GROUPS, LANES)
    flat = lax.psum_scatter(partial, CHIPS, scatter_dimension=0, tiled=True)
    sums = pl.pallas_call(
        unpack_kernel,
        out_shape=jax.ShapeDtypeStruct((rdev, BLOCK), jnp.float32),
        in_specs=[SMEM, VMEM],
        out_specs=VMEM,
        name="unpack",
    )(odd, flat)
    all_totals = everyones_sum(totals)[0]
    ref = lax.axis_index(("z", "y_hi"))
    my_totals = lax.dynamic_slice_in_dim(all_totals, ref * rdev, rdev, 0)
    return (sums, my_totals, evidence[:, 0])


def solution(mesh):
    fine = Mesh(mesh.devices.reshape(2, 4, 2, 8, 2), EVERYONE)
    placed = (
        P(EVERYONE, None),
        P(EVERYONE, None),
        P(("z", "y_hi"), None),
        P(),
        P(EVERYONE, None),
        P(EVERYONE),
    )
    return jax.shard_map(
        local,
        mesh=fine,
        in_specs=placed,
        out_specs=(P(("z", "y_hi"), ("y_lo", "x", "core")), P(("z", "y_hi")), P(EVERYONE)),
        check_vma=False,
    )
```

time: 1140 us -> 978 us (0.86)
  waiting for transfers between devices: 286 us -> 896 us
  other arithmetic: 280 us -> 1.38 us
  local copies, waits for them, and re-layouts: 297 us -> 23 us
  matrix products: 129 us -> 0 us
  blocking collectives: 93.9 us -> 0 us
  Pallas kernels: 0 us -> 18.9 us
    reduce_scatter x1, waiting for transfers between devices: 0.01 us -> 781 us  [local(): flat = lax.psum_scatter(partial, CHIPS, scatter_dimension=0, tiled=True)]
    ppermute x30 -> x11, waiting for transfers between devices: 286 us -> 16.2 us  [the longest x8 13.2 us: everyones_sum(): lax.ppermute(value, axis, [(i, i ^ bit) for i in range(count)])]
    reshape x16 -> x0, local copies, waits for them, and re-layouts: 166 us -> none  [back_rows(): gathered = gathered.reshape(count, trans, 2 * pixels)]
    dot_general x32 -> x0, matrix products: 129 us -> none  [the longest x16 66.1 us: back_rows(): lax.dot_general(columns, weighted, (((0,), (0,)), ((), ())), preferred_el...]
    reduce_sum x19 -> x0, other arithmetic: 103 us -> none  [the longest x16 102 us: back_rows(): sums_re = jnp.sum(gather_re * cosine[None] + gather_im * sine[None], axis=1)]
    all_gather x0 -> x1, waiting for transfers between devices: none -> 99.4 us  [local(): gathered = lax.all_gather(mine, CHIPS, axis=0, tiled=True)]
    psum x1 -> x0, blocking collectives: 93.9 us -> none  [local(): all_totals = lax.psum(jnp.sum(weights, axis=(0, 2)), ('dp', 'ref'))]
    cos x31 -> x0, other arithmetic: 89 us -> none  [phase_tables(): return (jnp.cos(angle), jnp.sin(angle))]
  transfers between devices with their start and end apart: 31 -> 13, of which waited for: 16 -> 12; matrix products, arithmetic and copies ran while one was open for 22% -> 0% of each run, Pallas kernels for 0% -> 1%
where the time goes in v1:
time: 978 us; the launch traced here: 975 us
  waiting for transfers between devices  896 us (92%)
  local copies, waits for them, and re-layouts  23 us (2%)
  starting transfers between devices  20.9 us (2%)
  Pallas kernels  18.9 us (2%)
  between operations  14.1 us (1%)
    reduce_scatter x1, waiting for transfers between devices, local(): flat = lax.psum_scatter(partial, CHIPS, scatter_dimension=0, tiled=True)  781 us
    all_gather x1, waiting for transfers between devices, local(): gathered = lax.all_gather(mine, CHIPS, axis=0, tiled=True)  99.4 us
    unnamed x20, local copies, waits for them, and re-layouts  23 us
  transfers between devices with their start and end apart: 13, of which 12 were waited for; matrix products, arithmetic and copies ran while one was open for 0% of the time, Pallas kernels for 1%

profile of v1, /device:TPU:1, one launch (start us, length us, event | category | flops | bytes accessed | tf_op | source)
XLA Modules:
  0.0 974.5 jit_solution(5162232184782557500)
XLA Ops:
  7.2 0.0 all-gather.2.cloned.1.call-start
  7.2 1.7 pack.1
  8.9 0.0 all-gather.2.cloned.1.call-update
  8.9 0.0 reduce-scatter.2.cloned.1.call-start
  9.0 0.0 copy-start.5
  9.0 1.4 copy-done.5
  10.4 0.0 copy-start.6
  10.4 1.1 copy-done.6
  11.5 0.3 weighted.1
  11.8 3.3 collective-permute-start
  15.2 0.8 copy.16.shifts_ref
  15.9 1.1 collective-permute-done.recv_ref
  17.1 5.6 rotate.1.rot_ref.args_3_
  22.7 0.0 copy-start
  22.7 5.0 copy-done
  27.7 99.4 %all-gather.2.cloned.1.call-done = bf16[12288,128]{1,0:T(8,128)(2,1)} async-done(((bf16[96,128]{1,0:T(8,128)(2,1)}), bf16[12288,128]{1,0:T(8,128)(2,1)}) %all-gather.2.cloned.1.call-update) | async-done | bytes 3145744 | tf_op jit(solution)/shard_map/all_gather | solution.py:243
  127.2 0.0 copy-start.1
  127.2 5.0 copy-done.1
  132.2 0.0 copy-start.4
  132.2 1.9 copy-done.4
  134.1 0.0 copy-start.7
  134.1 0.0 copy-start.8
  134.1 4.0 forward.1.args_0_
  138.1 4.8 collective-permute-start.1
  142.9 0.0 copy-done.7
  142.9 0.1 copy.17
  143.0 0.0 copy-done.8
  143.0 0.1 fusion
  143.0 0.1 collective-permute-start.2
  143.1 0.1 fusion.2
  143.2 1.8 collective-permute-done.2
  145.0 0.0 collective-permute-done.1.args_1_
  145.0 0.0 copy-start.2
  145.0 5.0 copy-done.2
  150.0 5.9 backward.1
  155.9 0.0 copy-start.3
  155.9 2.6 copy-done.3
  158.6 0.0 reduce-scatter.2.cloned.1.call-update
  158.6 0.5 collective-permute-start.3
  159.1 0.8 collective-permute-done.3
  159.9 1.2 collective-permute-start.4
  161.1 1.3 collective-permute-done.4
  162.3 2.8 collective-permute-start.5
  165.1 1.1 collective-permute-done.5
  166.2 1.0 collective-permute-start.6
  167.3 1.4 collective-permute-done.6
  168.7 2.5 collective-permute-start.7
  171.2 1.4 collective-permute-done.7
  172.6 0.3 collective-permute-start.8
  172.9 2.1 collective-permute-done.8
  175.0 1.8 collective-permute-start.9
  176.8 2.0 collective-permute-done.9
  178.7 2.6 collective-permute-start.10
  181.4 0.6 reduce
  182.0 3.1 collective-permute-done.10
  185.1 0.6 fusion.1
  185.7 780.6 %reduce-scatter.2.cloned.1.call-done.flat_ref = f32[96,128]{1,0:T(8,128)} async-done(((f32[12288,128]{1,0:T(8,128)}), f32[96,128]{1,0:T(8,128)}) %reduce-scatter.2.cloned.1.call-update) | async-done | bytes 49168 | tf_op jit(solution)/shard_map/reduce_scatter | solution.py:301
  966.3 1.4 unpack.1
  (8 shorter events, 0.0 us)
Async XLA Ops:
  7.2 120.0 %all-gather.2.cloned.1.call-start = ((), (), s32[]{:S(2)}) async-start(), calls=%async_computation.1 | async-start | bytes 3170304 | tf_op jit(solution)/shard_map/all_gather | solution.py:243
  8.9 957.4 %reduce-scatter.2.cloned.1.call-start = ((), (), s32[]{:S(2)}) async-start(), calls=%async_computation.2 | async-start | bytes 6340608 | tf_op jit(solution)/shard_map/reduce_scatter | solution.py:301
  9.0 1.4 copy-start.5
  10.4 1.1 copy-start.6
  11.8 5.2 collective-permute-start
  22.7 5.0 copy-start
  127.2 5.0 copy-start.1
  132.2 1.9 copy-start.4
  134.1 8.8 copy-start.7
  134.1 8.9 copy-start.8
  138.1 6.9 collective-permute-start.1
  143.0 1.9 collective-permute-start.2
  145.0 5.0 copy-start.2
  155.9 2.7 copy-start.3
  158.6 1.3 collective-permute-start.3
  159.9 2.4 collective-permute-start.4
  162.3 3.9 collective-permute-start.5
  166.2 2.4 collective-permute-start.6
  168.7 3.9 collective-permute-start.7
  172.6 2.4 collective-permute-start.8
  175.0 3.7 collective-permute-start.9
  178.7 6.3 collective-permute-start.10
Sparse Core Ops, SparseCore 0:
  12.2 114.8 all-gather.1
  158.7 807.5 reduce-scatter.1
